TPU v7x, 128 devices: a whole 4x4x4 slice. The times are simulated.
128 devices in a mesh: wide: 16 (over z, x), narrow: 8 (over y, core).
Axes of the slice: x: 4, y: 4, z: 4, core: 2. Of those that a mesh axis runs over, the one named last changes fastest.
Arguments:
- node_latent: float32 [32768, 512], P(('wide', 'narrow')), may hold values from -6 to 6
- edge_latent: float32 [131072, 512], P(('wide', 'narrow')), may hold values from -6 to 6
- edge_slot: int32 [131072], P(('wide', 'narrow')), may hold values from 0 to 1279, as said below
- edge_receiver: int32 [131072], P(('wide', 'narrow')), may hold values from 0 to 255
- send_rows: int32 [128, 128, 8], P(('wide', 'narrow')), may hold values from 0 to 255
- node_cotangent: float32 [32768, 512], P(('wide', 'narrow')), may hold values from -6 to 6
- edge_cotangent: float32 [131072, 512], P(('wide', 'narrow')), may hold values from -6 to 6
- edge_w1: float32 [1536, 512], replicated, may hold values from -0.15625 to 0.15625
- edge_b1: float32 [512], replicated, may hold values from -3 to 3
- edge_w2: float32 [512, 512], replicated, may hold values from -0.25 to 0.25
- edge_gain: float32 [512], replicated, may hold values from 0.1 to 1.9
- node_w1: float32 [1024, 512], replicated, may hold values from -0.1875 to 0.1875
- node_b1: float32 [512], replicated, may hold values from -3 to 3
- node_w2: float32 [512, 512], replicated, may hold values from -0.25 to 0.25
- node_gain: float32 [512], replicated, may hold values from 0.1 to 1.9
Outputs:
- new_nodes: float32 [32768, 512], P(('wide', 'narrow'))
- node_grad: float32 [32768, 512], P(('wide', 'narrow'))
- edge_grad: float32 [131072, 512], P(('wide', 'narrow'))
- edge_w1_grad: float32 [1536, 512], replicated
- edge_b1_grad: float32 [512], replicated
- edge_w2_grad: float32 [512, 512], replicated
- edge_gain_grad: float32 [512], replicated
- node_w1_grad: float32 [1024, 512], replicated
- node_b1_grad: float32 [512], replicated
- node_w2_grad: float32 [512, 512], replicated
- node_gain_grad: float32 [512], replicated
Inputs may be any that keep to these rules, and one draw needn't show every extreme that they name: `edge_slot`: of the 8 slots that one device sends to another, the edges of the receiving device read only the first k, k from 1 to 8 for each pair of devices; every device reads the last of the 8 slots of at least one other device. Slots that no edge reads still hold node indices.
All inputs are finite; a program needn't handle non-finite values.
Results may differ from a plain program's by a relative error of at most 0.000086.
Values sent between devices are 32-bit elements; how exact they have to be, the bound alone decides.
A program may use at most 128 MiB of HBM per device.

v0:
```python
import functools

import jax
import jax.numpy as jnp
from jax import lax
from jax.experimental import pallas as pl
from jax.experimental.pallas import tpu as pltpu
from jax.sharding import PartitionSpec as P

MESH = pl.DeviceIdType.MESH
F32, BF16, I32 = jnp.float32, jnp.bfloat16, jnp.int32
W = 512
NODES = 256
EDGES = 1024
SLOTS = 1280
CH = 256

FLAT = 15360
ROT = 5120
SIZE = (640, 160, 40)
HALF = (320, 80, 24)
ORDERS = ((0, 1, 2), (1, 2, 0), (2, 0, 1))
SEMS = 35
UNITS = {"nw1a": 0, "nw1b": 4, "nw2": 8, "w2": 12, "w1c": 16, "w1a": 20, "w1b": 24, "small": 28}
WROW = {"w1a": 0, "w1b": 512, "w1c": 1024, "w2": 1536, "nw1a": 2048, "nw1b": 2560, "nw2": 3072}


def coords():
    w = lax.axis_index("wide")
    n = lax.axis_index("narrow")
    return w % 4, n // 2, w // 4, n % 2


def device(x, y, z, c):
    return (z * 4 + x, y * 2 + c)


def wait(ref, sem):
    pltpu.make_async_copy(ref, ref, sem).wait()


def rows(start, n):
    return pl.ds(pl.multiple_of(start, 8), n)


def split(v):
    high = v.astype(BF16)
    return high, (v - high.astype(F32)).astype(BF16)


def dot(a, b):
    return jnp.dot(a, b, preferred_element_type=F32)


def dot_nt(a, b):
    return lax.dot_general(a, b, (((1,), (1,)), ((), ())), preferred_element_type=F32)


def dot_tn(a, b):
    return lax.dot_general(a, b, (((0,), (0,)), ((), ())), preferred_element_type=F32)


def three(op, a, b):
    return op(a[0], b[0]) + op(a[1], b[0]) + op(a[0], b[1])


def two(one_hot, pair):
    return dot(one_hot, pair[0]) + dot(one_hot, pair[1])


def reduce_rotation(rot, buf, out, halves_in, send, recv, started):
    here = coords()
    core = here[3]
    order = ORDERS[rot]
    pos = [here[a] for a in order]

    def shifted(stage, by):
        c = list(here)
        c[order[stage]] = (c[order[stage]] + by) % 4
        return device(*c)

    sibling = device(here[0], here[1], here[2], 1 - core)

    def post(src, dst, k, to):
        d = pltpu.make_async_remote_copy(
            src_ref=src,
            dst_ref=dst,
            send_sem=send.at[rot, k],
            recv_sem=recv.at[rot, k],
            device_id=to,
            device_id_type=MESH,
        )
        d.start()
        started.append(d)

    base = rot * ROT
    mine = base + core * 2560
    other = base + (1 - core) * 2560
    post(buf.at[rows(other, 2560)], out.at[rows(other, 2560)], 0, sibling)
    yield
    wait(out.at[rows(mine, 2560)], recv.at[rot, 0])

    def add(i, _):
        r = rows(mine + i * 320, 320)
        buf[r] = buf[r] + out[r]
        return 0

    lax.fori_loop(0, 8, add, 0)
    region = mine
    into = 0
    for s in range(3):
        L = SIZE[s]
        A = HALF[s]
        B = L - A
        j = pos[s]
        k = 1 + 6 * s
        at = lambda q, region=region, j=j, L=L: region + ((j + q) % 4) * L
        first_a, first_b = rows(into, A), rows(into + A, B)
        plus_a, plus_b = rows(into + L, A), rows(into + L + A, B)
        minus_a, minus_b = rows(into + 2 * L, A), rows(into + 2 * L + A, B)
        land = lambda r: halves_in.at[rot, r]
        up, down = shifted(s, 1), shifted(s, -1)
        post(buf.at[rows(at(2), A)], land(first_a), k, down)
        post(buf.at[rows(at(2) + A, B)], land(first_b), k + 1, up)
        post(buf.at[rows(at(-1) + A, B)], land(plus_b), k + 2, down)
        post(buf.at[rows(at(1), A)], land(minus_a), k + 3, up)
        yield
        wait(land(first_a), recv.at[rot, k])
        r = rows(at(-1), A)
        buf[r] = buf[r] + halves_in[rot, first_a]
        post(buf.at[r], land(plus_a), k + 4, down)
        wait(land(first_b), recv.at[rot, k + 1])
        r = rows(at(1) + A, B)
        buf[r] = buf[r] + halves_in[rot, first_b]
        post(buf.at[r], land(minus_b), k + 5, up)
        yield
        wait(land(plus_b), recv.at[rot, k + 2])
        wait(land(minus_a), recv.at[rot, k + 3])
        wait(land(plus_a), recv.at[rot, k + 4])
        wait(land(minus_b), recv.at[rot, k + 5])
        r = rows(at(0), L)
        total = buf[r] + halves_in[rot, rows(into + L, L)] + halves_in[rot, rows(into + 2 * L, L)]
        if s < 2:
            buf[r] = total
        else:
            out[r] = total
        region = region + j * L
        into += 3 * L
    for s in (2, 1, 0):
        L = SIZE[s]
        A = HALF[s]
        B = L - A
        j = pos[s]
        k = 19 + 4 * s
        region = region - j * L
        at = lambda q, region=region, j=j, L=L: region + ((j + q) % 4) * L
        up, down = shifted(s, 1), shifted(s, -1)
        own = out.at[rows(at(0), L)]
        post(own, own, k, up)
        post(own, own, k + 1, down)
        if s == 0:
            post(own, own, 31, sibling)
        yield
        left, right = out.at[rows(at(-1), L)], out.at[rows(at(1), L)]
        wait(left, recv.at[rot, k])
        part = out.at[rows(at(-1), A)]
        post(part, part, k + 2, up)
        if s == 0:
            post(left, left, 32, sibling)
        wait(right, recv.at[rot, k + 1])
        part = out.at[rows(at(1) + A, B)]
        post(part, part, k + 3, down)
        if s == 0:
            post(right, right, 33, sibling)
        yield
        wait(out.at[rows(at(2), A)], recv.at[rot, k + 2])
        wait(out.at[rows(at(2) + A, B)], recv.at[rot, k + 3])
    opposite = out.at[rows(at(2), L)]
    post(opposite, opposite, 34, sibling)
    yield
    for n in range(4):
        wait(out.at[rows(other, 640)], recv.at[rot, 31 + n])


def kernel(
    slot_ref, receiver_ref, list_ref, vector_ref,
    node_h, edge_h, ncot_h, ecot_h, w1_h, w2_h, nw1_h, nw2_h,
    new_nodes_h, node_grad_h, edge_grad_h, w1g_h, w2g_h, nw1g_h, nw2g_h, small_h,
    node_v, node_hi, node_lo, ncot, ecot, pre, whi, wlo, sbuf, rbuf, abuf,
    oslot, orecv, orecv_t, osend, osend_t, tabh, tabl, sh, sl, hh, hl, dph, dpl,
    rstd_v, agg, npre, carry, gloc, rsum, buf, out, halves_in,
    lsem, send1, recv1, send2, recv2, send, recv,
):
    x, y, z, c = coords()
    me = (z * 4 + x) * 8 + y * 2 + c

    def peer(d):
        return (z + d // 32) % 4 * 4 + (x + d // 8) % 4, (y + d // 2) % 4 * 2 + (c + d) % 2

    def load(src, dst, k):
        d = pltpu.make_async_copy(src, dst, lsem.at[k])
        d.start()
        return d

    xhat = rbuf
    load_node = load(node_h, node_v, 0)
    load_edge = load(edge_h, pre, 1)
    load_ncot = load(ncot_h, ncot, 2)
    blocks = [(w1_h, 0), (w1_h, 512), (w1_h, 1024), (w2_h, 0), (nw1_h, 0), (nw1_h, 512), (nw2_h, 0)]

    def load_weights(b):
        src, at = blocks[b]
        return load(src.at[pl.ds(at, 512)], ecot.at[pl.ds(b % 2 * 512, 512)], 3 + b)

    loading = {b: load_weights(b) for b in (0, 1)}
    barrier = pltpu.get_barrier_semaphore()

    def greet(i, _):
        pl.semaphore_signal(barrier, inc=1, device_id=peer(i), device_id_type=MESH)
        return 0

    lax.fori_loop(1, 128, greet, 0)

    def line(ref, i):
        return jnp.broadcast_to(ref[pl.ds(i, 1), :], (128, 128))

    def across(i, ref, store, n):
        lanes = lax.broadcasted_iota(I32, (128, 128), 1)
        column = line(ref, i).T
        for q in range(n // 128):
            store[rows(i * 128, 128), q * 128 : q * 128 + 128] = jnp.where(
                column == lanes + q * 128, 1.0, 0.0
            ).astype(BF16)

    def hot(i, _):
        across(i, list_ref, osend, NODES)
        return 0

    lax.fori_loop(0, 8, hot, 0)
    load_node.wait()
    nhi, nlo = split(node_v[...])
    node_hi[...] = nhi
    node_lo[...] = nlo

    def gather(i, _):
        r = rows(i * CH, CH)
        sbuf[r] = two(osend[r], (node_hi[...], node_lo[...]))
        return 0

    lax.fori_loop(0, EDGES // CH, gather, 0)
    mine8 = rows(me * 8, 8)
    rbuf[mine8] = sbuf[mine8]
    pl.semaphore_wait(barrier, 127)

    def send_rows(i, _):
        w, n = peer(i * 37 % 128)
        pltpu.make_async_remote_copy(
            src_ref=sbuf.at[rows((w * 8 + n) * 8, 8)],
            dst_ref=rbuf.at[mine8],
            send_sem=send1,
            recv_sem=recv1,
            device_id=(w, n),
            device_id_type=MESH,
        ).start()
        return 0

    lax.fori_loop(1, 128, send_rows, 0)

    for b in range(7):
        loading[b].wait()

        def cut(i, _, b=b):
            hi, lo = split(ecot[rows(b % 2 * 512 + i * 128, 128)])
            whi[rows(b * 512 + i * 128, 128)] = hi
            wlo[rows(b * 512 + i * 128, 128)] = lo
            return 0

        lax.fori_loop(0, 4, cut, 0)
        if b + 2 < 7:
            loading[b + 2] = load_weights(b + 2)
    load_ecot = load(ecot_h, ecot, 10)

    def weight(name):
        r = pl.ds(WROW[name], 512)
        return whi[r], wlo[r]

    def hot_edges(i, _):
        across(i, slot_ref, oslot, SLOTS)
        across(i, receiver_ref, orecv, NODES)
        return 0

    lax.fori_loop(0, 8, hot_edges, 0)

    def down(ref, i, first, n):
        return jnp.where(
            jnp.broadcast_to(ref[pl.ds(i, 1), :], (n, 128))
            == lax.broadcasted_iota(I32, (n, 128), 0) + first,
            1.0,
            0.0,
        ).astype(BF16)

    for i in range(8):
        lanes = slice(i % 2 * 128, i % 2 * 128 + 128)
        orecv_t[i // 2, :, lanes] = down(receiver_ref, i, 0, NODES)
        osend_t[i // 2, :, lanes] = down(list_ref, i, 0, NODES)

    node_pair = lambda: (node_hi[...], node_lo[...])
    projected = split(three(dot, node_pair(), weight("w1c")))
    agg[...] = projected[0].astype(F32)
    gloc[...] = projected[1].astype(F32)
    npre[...] = three(dot, node_pair(), weight("nw1a")) + vector_ref[2:3, :]
    load_edge.wait()

    def first_layer(i, _):
        r = rows(i * CH, CH)
        pair = split(pre[r])
        pre[r] = (
            three(dot, pair, weight("w1a"))
            + two(orecv[r], (agg[...].astype(BF16), gloc[...].astype(BF16)))
            + vector_ref[0:1, :]
        )
        return 0

    lax.fori_loop(0, EDGES // CH, first_layer, 0)
    tabh[0:NODES] = node_hi[...]
    tabl[0:NODES] = node_lo[...]
    agg[...] = jnp.zeros_like(agg)

    wait(rbuf.at[pl.ds(0, 1016)], recv1)
    wait(sbuf.at[pl.ds(0, 1016)], send1)

    def cut_table(i, _):
        hi, lo = split(rbuf[rows(i * 256, 256)])
        tabh[rows(256 + i * 256, 256)] = hi
        tabl[rows(256 + i * 256, 256)] = lo
        return 0

    lax.fori_loop(0, 4, cut_table, 0)

    def forward(i, _):
        r = rows(i * CH, CH)
        hot = oslot[r, 0:SLOTS]
        senders = dot(hot, tabh[...]).astype(BF16), dot(hot, tabl[...]).astype(BF16)
        sh[r] = senders[0]
        sl[r] = senders[1]
        v = pre[r] + three(dot, senders, weight("w1b"))
        s = 1.0 / (1.0 + jnp.exp(-v))
        pre[r] = s * (1.0 + v * (1.0 - s))
        hidden = split(v * s)
        hh[r] = hidden[0]
        hl[r] = hidden[1]
        zed = three(dot, hidden, weight("w2"))
        centre = zed - jnp.mean(zed, axis=1, keepdims=True)
        rstd = lax.rsqrt(jnp.mean(centre * centre, axis=1, keepdims=True) + 1e-05)
        scaled = centre * rstd
        xhat[r] = scaled
        rstd_v[r] = jnp.broadcast_to(rstd, (CH, 128))
        agg[...] += two(orecv_t[i], split(scaled))
        return 0

    lax.fori_loop(0, EDGES // CH, forward, 0)

    aggregate = split(agg[...] * vector_ref[1:2, :])
    v = npre[...] + three(dot, aggregate, weight("nw1b"))
    s = 1.0 / (1.0 + jnp.exp(-v))
    slope = s * (1.0 + v * (1.0 - s))
    hidden = split(v * s)
    zed = three(dot, hidden, weight("nw2"))
    centre = zed - jnp.mean(zed, axis=1, keepdims=True)
    rstd = lax.rsqrt(jnp.mean(centre * centre, axis=1, keepdims=True) + 1e-05)
    scaled = centre * rstd
    npre[...] = node_v[...] + scaled * vector_ref[3:4, :]
    store_nodes = load(npre, new_nodes_h, 11)
    load_ncot.wait()
    ngain_grad = jnp.sum(ncot[...] * scaled, axis=0, keepdims=True)
    cot = ncot[...] * vector_ref[3:4, :]
    dz = split(
        rstd
        * (
            cot
            - jnp.mean(cot, axis=1, keepdims=True)
            - scaled * jnp.mean(cot * scaled, axis=1, keepdims=True)
        )
    )
    dpre = three(dot_nt, dz, weight("nw2")) * slope
    nb1_grad = jnp.sum(dpre, axis=0, keepdims=True)
    dpre = split(dpre)
    dagg = split(three(dot_nt, dpre, weight("nw1b")))
    ncot[...] += three(dot_nt, dpre, weight("nw1a"))

    def put(unit, value, first=0):
        for q in range(4):
            buf[rows((unit + q) * 512 + first, value.shape[0])] = value[:, q * 128 : q * 128 + 128]

    put(UNITS["nw2"], three(dot_tn, hidden, dz))
    put(UNITS["nw1a"], three(dot_tn, node_pair(), dpre))
    put(UNITS["nw1b"], three(dot_tn, aggregate, dpre))
    started = []
    rotations = [
        reduce_rotation(r, buf, out, halves_in, send, recv, started) for r in range(3)
    ]
    next(rotations[0])

    load_ecot.wait()
    carry[...] = jnp.zeros_like(carry)
    agg[...] = dagg[0].astype(F32)
    gloc[...] = dagg[1].astype(F32)

    def backward(i, _):
        r = rows(i * CH, CH)
        scaled = xhat[r]
        mcot = ecot[r] + two(orecv[r], (agg[...].astype(BF16), gloc[...].astype(BF16)))
        carry[0:1] += jnp.sum(mcot * scaled, axis=0, keepdims=True)
        cot = mcot * vector_ref[1:2, :]
        dz = split(
            rstd_v[r][:, 0:1]
            * (
                cot
                - jnp.mean(cot, axis=1, keepdims=True)
                - scaled * jnp.mean(cot * scaled, axis=1, keepdims=True)
            )
        )
        tabh[r] = dz[0]
        tabl[r] = dz[1]
        dpre = three(dot_nt, dz, weight("w2")) * pre[r]
        carry[1:2] += jnp.sum(dpre, axis=0, keepdims=True)
        dpre = split(dpre)
        dph[r] = dpre[0]
        dpl[r] = dpre[1]
        return 0

    lax.fori_loop(0, EDGES // CH, backward, 0)
    next(rotations[0])
    load_edge = load(edge_h, pre, 12)

    def scatter(first):
        for i in range(8):
            oslot[0:256, i * 128 : i * 128 + 128] = down(slot_ref, i, first, 256)
        return two(oslot[0:256, 0:EDGES], (dph[...], dpl[...]))

    def plane(n, _):
        dz_ = (n + 1) % 4
        at = (z + dz_) % 4 * 256
        sbuf[rows(at, 256)] = scatter(NODES + at)

        def give(i, _):
            w, nn = peer(dz_ * 32 + i * 13 % 32)
            pltpu.make_async_remote_copy(
                src_ref=sbuf.at[rows((w * 8 + nn) * 8, 8)],
                dst_ref=abuf.at[mine8],
                send_sem=send2,
                recv_sem=recv2,
                device_id=(w, nn),
                device_id_type=MESH,
            ).start()
            return 0

        lax.fori_loop(jnp.where(dz_ == 0, 1, 0), 32, give, 0)
        return 0

    lax.fori_loop(0, 4, plane, 0)
    next(rotations[0])
    abuf[mine8] = sbuf[mine8]
    gloc[...] = scatter(0)
    rsum[...] = sum(
        two(orecv_t[i], (dph[pl.ds(i * CH, CH)], dpl[pl.ds(i * CH, CH)])) for i in range(4)
    )

    def tall(unit, a, b, n):
        def part(i, _):
            lanes = pl.ds(pl.multiple_of(i * 128, 128), 128)
            value = (
                dot_tn(a[0][:, lanes], b[0][pl.ds(0, n)])
                + dot_tn(a[1][:, lanes], b[0][pl.ds(0, n)])
                + dot_tn(a[0][:, lanes], b[1][pl.ds(0, n)])
            )
            put(unit, value, i * 128)
            return 0

        lax.fori_loop(0, 4, part, 0)

    tall(UNITS["w2"], (hh, hl), (tabh, tabl), EDGES)
    rcut = split(rsum[...])
    put(UNITS["w1c"], three(dot_tn, node_pair(), rcut))
    next(rotations[0])
    next(rotations[1])
    tall(UNITS["w1b"], (sh, sl), (dph, dpl), EDGES)
    load_edge.wait()

    def cut_edges(i, _):
        r = rows(i * 128, 128)
        hi, lo = split(pre[r])
        hh[r] = hi
        hl[r] = lo
        return 0

    lax.fori_loop(0, 8, cut_edges, 0)
    tall(UNITS["w1a"], (hh, hl), (dph, dpl), EDGES)
    vectors = jnp.concatenate(
        [carry[1:2], carry[0:1], nb1_grad, ngain_grad, jnp.zeros((4, W), F32)], axis=0
    )
    small = UNITS["small"] * 512
    buf[small : small + 1024] = jnp.zeros((1024, 128), F32)
    for q in range(4):
        buf[small + 8 * q : small + 8 * q + 8] = vectors[:, q * 128 : q * 128 + 128]
    next(rotations[2])

    def edge_out(i, _):
        r = rows(i * CH, CH)
        ecot[r] += three(dot_nt, (dph[r], dpl[r]), weight("w1a"))
        return 0

    lax.fori_loop(0, EDGES // CH, edge_out, 0)
    store_edges = load(ecot, edge_grad_h, 13)
    ncot[...] += three(dot_nt, rcut, weight("w1c"))

    live = list(rotations)

    def step():
        for t in list(live):
            if next(t, 0) == 0:
                live.remove(t)

    for _ in range(BEFORE):
        step()
    wait(abuf.at[pl.ds(0, 1016)], recv2)

    def collect(i, _):
        gloc[...] += two(osend_t[i], split(abuf[rows(i * 256, 256)]))
        return 0

    lax.fori_loop(0, 4, collect, 0)
    ncot[...] += three(dot_nt, split(gloc[...]), weight("w1b"))
    store_grad = load(ncot, node_grad_h, 14)
    while live:
        step()
    stores = [store_nodes, store_edges, store_grad]
    k = 15
    for name, ref, at in (
        ("w1a", w1g_h, 0),
        ("w1b", w1g_h, 512),
        ("w1c", w1g_h, 1024),
        ("w2", w2g_h, 0),
        ("nw1a", nw1g_h, 0),
        ("nw1b", nw1g_h, 512),
        ("nw2", nw2g_h, 0),
    ):
        for q in range(4):
            src = out.at[pl.ds((UNITS[name] + q) * 512, 512)]
            stores.append(load(src, ref.at[pl.ds(at, 512), pl.ds(q * 128, 128)], k))
            k += 1
    for q in range(4):
        stores.append(load(out.at[pl.ds(small + 8 * q, 8)], small_h.at[:, pl.ds(q * 128, 128)], k))
        k += 1
    wait(sbuf.at[pl.ds(0, 1016)], send2)
    for d in started:
        d.wait_send()
    for d in stores:
        d.wait()


BEFORE = 4


def local(
    node_latent,
    edge_latent,
    edge_slot,
    edge_receiver,
    send_rows,
    node_cotangent,
    edge_cotangent,
    edge_w1,
    edge_b1,
    edge_w2,
    edge_gain,
    node_w1,
    node_b1,
    node_w2,
    node_gain,
):
    vectors = jnp.stack([edge_b1, edge_gain, node_b1, node_gain])
    shape = lambda *s: jax.ShapeDtypeStruct(s, F32)
    v32 = lambda *s: pltpu.VMEM(s, F32)
    v16 = lambda *s: pltpu.VMEM(s, BF16)
    anywhere = pl.BlockSpec(memory_space=pl.ANY)
    near = pl.BlockSpec(memory_space=pltpu.VMEM)
    result = pl.pallas_call(
        kernel,
        out_shape=(
            shape(NODES, W),
            shape(NODES, W),
            shape(EDGES, W),
            shape(1536, W),
            shape(512, W),
            shape(1024, W),
            shape(512, W),
            shape(8, W),
        ),
        in_specs=[near] * 4 + [anywhere] * 8,
        out_specs=[anywhere] * 8,
        scratch_shapes=[
            v32(NODES, W),
            v16(NODES, W),
            v16(NODES, W),
            v32(NODES, W),
            v32(EDGES, W),
            v32(EDGES, W),
            v16(3584, W),
            v16(3584, W),
            v32(EDGES, W),
            v32(EDGES, W),
            v32(EDGES, W),
            v16(EDGES, SLOTS),
            v16(EDGES, NODES),
            v16(4, NODES, 256),
            v16(EDGES, NODES),
            v16(4, NODES, 256),
            v16(SLOTS, W),
            v16(SLOTS, W),
            v16(EDGES, W),
            v16(EDGES, W),
            v16(EDGES, W),
            v16(EDGES, W),
            v16(EDGES, W),
            v16(EDGES, W),
            v32(EDGES, 128),
            v32(NODES, W),
            v32(NODES, W),
            v32(8, W),
            v32(NODES, W),
            v32(NODES, W),
            v32(FLAT, 128),
            v32(FLAT, 128),
            v32(3, 2520, 128),
            pltpu.SemaphoreType.DMA((48,)),
            pltpu.SemaphoreType.DMA,
            pltpu.SemaphoreType.DMA,
            pltpu.SemaphoreType.DMA,
            pltpu.SemaphoreType.DMA,
            pltpu.SemaphoreType.DMA((3, SEMS)),
            pltpu.SemaphoreType.DMA((3, SEMS)),
        ],
        compiler_params=pltpu.CompilerParams(
            collective_id=1, has_side_effects=True, vmem_limit_bytes=63 << 20
        ),
    )(
        edge_slot.reshape(8, 128),
        edge_receiver.reshape(8, 128),
        send_rows.reshape(8, 128),
        vectors,
        node_latent,
        edge_latent,
        node_cotangent,
        edge_cotangent,
        edge_w1,
        edge_w2,
        node_w1,
        node_w2,
    )
    new_nodes, node_grad, edge_grad, w1g, w2g, nw1g, nw2g, small = result
    return (
        new_nodes,
        node_grad,
        edge_grad,
        w1g,
        small[0],
        w2g,
        small[1],
        nw1g,
        small[2],
        nw2g,
        small[3],
    )


def solution(mesh):
    return jax.shard_map(
        local,
        mesh=mesh,
        in_specs=(
            P(("wide", "narrow"), None),
            P(("wide", "narrow"), None),
            P(("wide", "narrow")),
            P(("wide", "narrow")),
            P(("wide", "narrow"), None, None),
            P(("wide", "narrow"), None),
            P(("wide", "narrow"), None),
            P(),
            P(),
            P(),
            P(),
            P(),
            P(),
            P(),
            P(),
        ),
        out_specs=(
            P(("wide", "narrow"), None),
            P(("wide", "narrow"), None),
            P(("wide", "narrow"), None),
            P(),
            P(),
            P(),
            P(),
            P(),
            P(),
            P(),
            P(),
        ),
        check_vma=False,
    )
```

profile of v0, /device:TPU:1, one launch (start us, length us, event | category | flops | bytes accessed | tf_op | source)
XLA Modules:
  0.0 191.4 jit_solution(3524206075140545286)
XLA Ops:
  0.6 1.3 pad_maximum_fusion.vector_ref
  2.0 0.8 copy.27
  2.8 0.7 reshape.33.list_ref
  3.5 173.1 %shard_map.230 = (f32[256,512]{1,0:T(8,128)}, f32[256,512]{1,0:T(8,128)}, f32[1024,512]{1,0:T(8,128)}, f32[1536,512]{1,0:T(8,128)}, f32[512,512]{1,0:T(8,128)}, ...) custom-call(s32[8,128]{1,0:T(8,128)} %bitcast.10, s32[8,128]{1,0:T(8,128)} %bitcast.11, ...), custom_call_target="tpu_custom_call" | custom-call | tf_op jit(solution)/shard_map/pallas_call | solution.py:588
  176.6 0.0 copy-start.2
  176.6 1.5 fusion
  178.1 1.9 copy.35
  180.0 1.9 copy.36
  181.9 0.0 copy-done.2
  181.9 0.0 copy-start
  181.9 1.3 copy.37
  183.2 1.3 copy-done
  184.5 0.0 copy-start.4
  184.5 1.7 copy.38
  186.2 0.3 copy-done.4
  186.5 0.0 copy-start.1
  186.5 1.0 copy.39
  187.4 1.0 copy-done.1
  188.4 0.0 copy-start.3
  188.4 1.3 copy.40
  189.8 0.6 copy-done.3
  190.4 1.0 copy.41
Async XLA Ops:
  176.6 5.3 %copy-start.2 = (f32[1024,512]{1,0:T(8,128)S(1)}, f32[1024,512]{1,0:T(8,128)}, u32[]{:S(2)}) copy-start(f32[1024,512]{1,0:T(8,128)} %get-tuple-element.44) | copy-start | bytes 6291460
  181.9 2.6 %copy-start = (f32[1536,512]{1,0:T(8,128)S(1)}, f32[1536,512]{1,0:T(8,128)}, u32[]{:S(2)}) copy-start(f32[1536,512]{1,0:T(8,128)} %get-tuple-element.45) | copy-start | bytes 9437188
  184.5 2.0 %copy-start.4 = (f32[512,512]{1,0:T(8,128)S(1)}, f32[512,512]{1,0:T(8,128)}, u32[]{:S(2)}) copy-start(f32[512,512]{1,0:T(8,128)} %get-tuple-element.47) | copy-start | bytes 3145732
  186.5 2.0 %copy-start.1 = (f32[1024,512]{1,0:T(8,128)S(1)}, f32[1024,512]{1,0:T(8,128)}, u32[]{:S(2)}) copy-start(f32[1024,512]{1,0:T(8,128)} %get-tuple-element.49) | copy-start | bytes 6291460
  188.4 2.0 %copy-start.3 = (f32[512,512]{1,0:T(8,128)S(1)}, f32[512,512]{1,0:T(8,128)}, u32[]{:S(2)}) copy-start(f32[512,512]{1,0:T(8,128)} %get-tuple-element.51) | copy-start | bytes 3145732
where the time goes:
time: 192 us; the launch traced here: 191 us
  Pallas kernels  173 us (90%)
  local copies, waits for them, and re-layouts  16.2 us (8%)
    pallas_call x1, Pallas kernels, local(): pl.pallas_call(kernel, out_shape=(shape(NODES, W), shape(NODES, W), shape...  173 us
    unnamed x18, local copies, waits for them, and re-layouts  14 us

commit v1 on v0

--- a/solution.py
+++ b/solution.py
@@ -16,12 +16,17 @@
 CH = 256
 
 FLAT = 15360
-ROT = 5120
-SIZE = (640, 160, 40)
-HALF = (320, 80, 24)
 ORDERS = ((0, 1, 2), (1, 2, 0), (2, 0, 1))
-SEMS = 35
-UNITS = {"nw1a": 0, "nw1b": 4, "nw2": 8, "w2": 12, "w1c": 16, "w1a": 20, "w1b": 24, "small": 28}
+SEMS = 30
+PARTS = (
+    (0, 0, 16, 0),
+    (1, 2048, 16, 1008),
+    (2, 4096, 16, 2016),
+    (0, 6144, 24, 3024),
+    (1, 9216, 24, 4536),
+    (2, 12288, 24, 6048),
+)
+UNITS = {"nw2": 0, "nw1a": 4, "nw1b": 8, "w2": 12, "w1c": 16, "w1b": 20, "w1a": 24, "small": 28}
 WROW = {"w1a": 0, "w1b": 512, "w1c": 1024, "w2": 1536, "nw1a": 2048, "nw1b": 2560, "nw2": 3072}
 
 
@@ -68,11 +73,13 @@
     return dot(one_hot, pair[0]) + dot(one_hot, pair[1])
 
 
-def reduce_rotation(rot, buf, out, halves_in, send, recv, started):
+def reduce_part(part, buf, out, halves_in, send, recv, started):
+    rot, base, leaf, into = PARTS[part]
     here = coords()
     core = here[3]
     order = ORDERS[rot]
     pos = [here[a] for a in order]
+    sizes = (16 * leaf, 4 * leaf, leaf)
 
     def shifted(stage, by):
         c = list(here)
@@ -85,108 +92,131 @@
         d = pltpu.make_async_remote_copy(
             src_ref=src,
             dst_ref=dst,
-            send_sem=send.at[rot, k],
-            recv_sem=recv.at[rot, k],
+            send_sem=send.at[part, k],
+            recv_sem=recv.at[part, k],
             device_id=to,
             device_id_type=MESH,
         )
         d.start()
         started.append(d)
 
-    base = rot * ROT
-    mine = base + core * 2560
-    other = base + (1 - core) * 2560
-    post(buf.at[rows(other, 2560)], out.at[rows(other, 2560)], 0, sibling)
+    mine = base + core * 64 * leaf
+    other = base + (1 - core) * 64 * leaf
+    L = sizes[0]
+    A = L // 2
+    j = pos[0]
+    spot = lambda q: mine + ((j + q) % 4) * L
+    for m, q in enumerate((2, -1, 1, 0)):
+        r = rows(other + ((j + q) % 4) * L, L)
+        post(buf.at[r], out.at[r], m, sibling)
     yield
-    wait(out.at[rows(mine, 2560)], recv.at[rot, 0])
-
-    def add(i, _):
-        r = rows(mine + i * 320, 320)
-        buf[r] = buf[r] + out[r]
-        return 0
-
-    lax.fori_loop(0, 8, add, 0)
-    region = mine
-    into = 0
-    for s in range(3):
-        L = SIZE[s]
-        A = HALF[s]
-        B = L - A
+
+    def core_add(m, q):
+        wait(out.at[rows(spot(q), L)], recv.at[part, m])
+
+        def add(i, _):
+            r = rows(spot(q) + i * A, A)
+            buf[r] = buf[r] + out[r]
+            return 0
+
+        lax.fori_loop(0, 2, add, 0)
+
+    up, down = shifted(0, 1), shifted(0, -1)
+    first_a, first_b = rows(into, A), rows(into + A, A)
+    plus_a, plus_b = rows(into + L, A), rows(into + L + A, A)
+    minus_a, minus_b = rows(into + 2 * L, A), rows(into + 2 * L + A, A)
+    land = lambda r: halves_in.at[r]
+    core_add(0, 2)
+    post(buf.at[rows(spot(2), A)], land(first_a), 4, down)
+    post(buf.at[rows(spot(2) + A, A)], land(first_b), 5, up)
+    core_add(1, -1)
+    post(buf.at[rows(spot(-1) + A, A)], land(plus_b), 6, down)
+    core_add(2, 1)
+    post(buf.at[rows(spot(1), A)], land(minus_a), 7, up)
+    yield
+    wait(land(first_a), recv.at[part, 4])
+    r = rows(spot(-1), A)
+    buf[r] = buf[r] + halves_in[first_a]
+    post(buf.at[r], land(plus_a), 8, down)
+    wait(land(first_b), recv.at[part, 5])
+    r = rows(spot(1) + A, A)
+    buf[r] = buf[r] + halves_in[first_b]
+    post(buf.at[r], land(minus_b), 9, up)
+    yield
+    core_add(3, 0)
+    wait(land(plus_b), recv.at[part, 6])
+    wait(land(minus_a), recv.at[part, 7])
+    wait(land(plus_a), recv.at[part, 8])
+    wait(land(minus_b), recv.at[part, 9])
+    r = rows(spot(0), L)
+    buf[r] = buf[r] + halves_in[rows(into + L, L)] + halves_in[rows(into + 2 * L, L)]
+    region = mine + j * L
+    into += 3 * L
+    for s in (1, 2):
+        L = sizes[s]
         j = pos[s]
-        k = 1 + 6 * s
-        at = lambda q, region=region, j=j, L=L: region + ((j + q) % 4) * L
-        first_a, first_b = rows(into, A), rows(into + A, B)
-        plus_a, plus_b = rows(into + L, A), rows(into + L + A, B)
-        minus_a, minus_b = rows(into + 2 * L, A), rows(into + 2 * L + A, B)
-        land = lambda r: halves_in.at[rot, r]
-        up, down = shifted(s, 1), shifted(s, -1)
-        post(buf.at[rows(at(2), A)], land(first_a), k, down)
-        post(buf.at[rows(at(2) + A, B)], land(first_b), k + 1, up)
-        post(buf.at[rows(at(-1) + A, B)], land(plus_b), k + 2, down)
-        post(buf.at[rows(at(1), A)], land(minus_a), k + 3, up)
+        k = 10 + 3 * (s - 1)
+        for m, q in enumerate((2, 1, 3)):
+            post(
+                buf.at[rows(region + ((j + q) % 4) * L, L)],
+                land(rows(into + m * L, L)),
+                k + m,
+                shifted(s, q),
+            )
         yield
-        wait(land(first_a), recv.at[rot, k])
-        r = rows(at(-1), A)
-        buf[r] = buf[r] + halves_in[rot, first_a]
-        post(buf.at[r], land(plus_a), k + 4, down)
-        wait(land(first_b), recv.at[rot, k + 1])
-        r = rows(at(1) + A, B)
-        buf[r] = buf[r] + halves_in[rot, first_b]
-        post(buf.at[r], land(minus_b), k + 5, up)
-        yield
-        wait(land(plus_b), recv.at[rot, k + 2])
-        wait(land(minus_a), recv.at[rot, k + 3])
-        wait(land(plus_a), recv.at[rot, k + 4])
-        wait(land(minus_b), recv.at[rot, k + 5])
-        r = rows(at(0), L)
-        total = buf[r] + halves_in[rot, rows(into + L, L)] + halves_in[rot, rows(into + 2 * L, L)]
-        if s < 2:
+        for m in range(3):
+            wait(land(rows(into + m * L, L)), recv.at[part, k + m])
+        r = rows(region + j * L, L)
+        total = buf[r] + halves_in[rows(into, L)]
+        total = total + halves_in[rows(into + L, L)] + halves_in[rows(into + 2 * L, L)]
+        if s == 1:
             buf[r] = total
         else:
             out[r] = total
         region = region + j * L
         into += 3 * L
-    for s in (2, 1, 0):
-        L = SIZE[s]
-        A = HALF[s]
-        B = L - A
+    for s in (2, 1):
+        L = sizes[s]
         j = pos[s]
-        k = 19 + 4 * s
+        k = 16 + 3 * (2 - s)
+        own = out.at[rows(region, L)]
+        for m, q in enumerate((2, 1, 3)):
+            post(own, own, k + m, shifted(s, q))
+        yield
         region = region - j * L
-        at = lambda q, region=region, j=j, L=L: region + ((j + q) % 4) * L
-        up, down = shifted(s, 1), shifted(s, -1)
-        own = out.at[rows(at(0), L)]
-        post(own, own, k, up)
-        post(own, own, k + 1, down)
-        if s == 0:
-            post(own, own, 31, sibling)
-        yield
-        left, right = out.at[rows(at(-1), L)], out.at[rows(at(1), L)]
-        wait(left, recv.at[rot, k])
-        part = out.at[rows(at(-1), A)]
-        post(part, part, k + 2, up)
-        if s == 0:
-            post(left, left, 32, sibling)
-        wait(right, recv.at[rot, k + 1])
-        part = out.at[rows(at(1) + A, B)]
-        post(part, part, k + 3, down)
-        if s == 0:
-            post(right, right, 33, sibling)
-        yield
-        wait(out.at[rows(at(2), A)], recv.at[rot, k + 2])
-        wait(out.at[rows(at(2) + A, B)], recv.at[rot, k + 3])
-    opposite = out.at[rows(at(2), L)]
-    post(opposite, opposite, 34, sibling)
+        for m, q in enumerate((2, 3, 1)):
+            wait(out.at[rows(region + ((j + q) % 4) * L, L)], recv.at[part, k + m])
+    L = sizes[0]
+    j = pos[0]
+    own = out.at[rows(spot(0), L)]
+    post(own, own, 22, up)
+    post(own, own, 23, down)
+    post(own, own, 26, sibling)
+    yield
+    left, right = out.at[rows(spot(-1), L)], out.at[rows(spot(1), L)]
+    wait(left, recv.at[part, 22])
+    piece = out.at[rows(spot(-1), A)]
+    post(piece, piece, 24, up)
+    post(left, left, 27, sibling)
+    wait(right, recv.at[part, 23])
+    piece = out.at[rows(spot(1) + A, A)]
+    post(piece, piece, 25, down)
+    post(right, right, 28, sibling)
+    yield
+    wait(out.at[rows(spot(2), A)], recv.at[part, 24])
+    wait(out.at[rows(spot(2) + A, A)], recv.at[part, 25])
+    opposite = out.at[rows(spot(2), L)]
+    post(opposite, opposite, 29, sibling)
     yield
     for n in range(4):
-        wait(out.at[rows(other, 640)], recv.at[rot, 31 + n])
+        wait(out.at[rows(other, L)], recv.at[part, 26 + n])
 
 
 def kernel(
-    slot_ref, receiver_ref, list_ref, vector_ref,
+    slot_ref, receiver_ref, list_ref, eb1_h, eg_h, nb1_h, ng_h,
     node_h, edge_h, ncot_h, ecot_h, w1_h, w2_h, nw1_h, nw2_h,
-    new_nodes_h, node_grad_h, edge_grad_h, w1g_h, w2g_h, nw1g_h, nw2g_h, small_h,
-    node_v, node_hi, node_lo, ncot, ecot, pre, whi, wlo, sbuf, rbuf, abuf,
+    new_nodes_h, node_grad_h, edge_grad_h, flat_h,
+    vector_ref, node_v, node_hi, node_lo, ncot, ecot, pre, whi, wlo, sbuf, rbuf, abuf,
     oslot, orecv, orecv_t, osend, osend_t, tabh, tabl, sh, sl, hh, hl, dph, dpl,
     rstd_v, agg, npre, carry, gloc, rsum, buf, out, halves_in,
     lsem, send1, recv1, send2, recv2, send, recv,
@@ -204,6 +234,9 @@
 
     xhat = rbuf
     load_node = load(node_h, node_v, 0)
+    load_vectors = [
+        load(ref, vector_ref.at[i], 21 + i) for i, ref in enumerate((eb1_h, eg_h, nb1_h, ng_h))
+    ]
     load_edge = load(edge_h, pre, 1)
     load_ncot = load(ncot_h, ncot, 2)
     blocks = [(w1_h, 0), (w1_h, 512), (w1_h, 1024), (w2_h, 0), (nw1_h, 0), (nw1_h, 512), (nw2_h, 0)]
@@ -216,10 +249,13 @@
     barrier = pltpu.get_barrier_semaphore()
 
     def greet(i, _):
+        for q in range(8):
+            pl.semaphore_signal(barrier, inc=1, device_id=peer(i * 8 + q), device_id_type=MESH)
+        return 0
+
+    for i in range(1, 8):
         pl.semaphore_signal(barrier, inc=1, device_id=peer(i), device_id_type=MESH)
-        return 0
-
-    lax.fori_loop(1, 128, greet, 0)
+    lax.fori_loop(1, 16, greet, 0)
 
     def line(ref, i):
         return jnp.broadcast_to(ref[pl.ds(i, 1), :], (128, 128))
@@ -238,6 +274,8 @@
 
     lax.fori_loop(0, 8, hot, 0)
     load_node.wait()
+    for d in load_vectors:
+        d.wait()
     nhi, nlo = split(node_v[...])
     node_hi[...] = nhi
     node_lo[...] = nlo
@@ -338,7 +376,7 @@
     lax.fori_loop(0, 4, cut_table, 0)
 
     def forward(i, _):
-        r = rows(i * CH, CH)
+        r = rows(i * 512, 512)
         hot = oslot[r, 0:SLOTS]
         senders = dot(hot, tabh[...]).astype(BF16), dot(hot, tabl[...]).astype(BF16)
         sh[r] = senders[0]
@@ -354,11 +392,13 @@
         rstd = lax.rsqrt(jnp.mean(centre * centre, axis=1, keepdims=True) + 1e-05)
         scaled = centre * rstd
         xhat[r] = scaled
-        rstd_v[r] = jnp.broadcast_to(rstd, (CH, 128))
-        agg[...] += two(orecv_t[i], split(scaled))
-        return 0
-
-    lax.fori_loop(0, EDGES // CH, forward, 0)
+        rstd_v[r] = jnp.broadcast_to(rstd, (512, 128))
+        pair = split(scaled)
+        agg[...] += two(orecv_t[2 * i], (pair[0][:256], pair[1][:256]))
+        agg[...] += two(orecv_t[2 * i + 1], (pair[0][256:], pair[1][256:]))
+        return 0
+
+    lax.fori_loop(0, 2, forward, 0)
 
     aggregate = split(agg[...] * vector_ref[1:2, :])
     v = npre[...] + three(dot, aggregate, weight("nw1b"))
@@ -386,7 +426,6 @@
     nb1_grad = jnp.sum(dpre, axis=0, keepdims=True)
     dpre = split(dpre)
     dagg = split(three(dot_nt, dpre, weight("nw1b")))
-    ncot[...] += three(dot_nt, dpre, weight("nw1a"))
 
     def put(unit, value, first=0):
         for q in range(4):
@@ -396,10 +435,34 @@
     put(UNITS["nw1a"], three(dot_tn, node_pair(), dpre))
     put(UNITS["nw1b"], three(dot_tn, aggregate, dpre))
     started = []
-    rotations = [
-        reduce_rotation(r, buf, out, halves_in, send, recv, started) for r in range(3)
-    ]
-    next(rotations[0])
+    parts = [reduce_part(p, buf, out, halves_in, send, recv, started) for p in range(6)]
+    stores = [store_nodes]
+    due = list(range(6))
+
+    def step(first, last):
+        for p in range(first, last):
+            if p in due and next(parts[p], 0) == 0:
+                due.remove(p)
+                r = pl.ds(PARTS[p][1], 128 * PARTS[p][2])
+                stores.append(load(out.at[r], flat_h.at[r], 15 + p))
+
+    def act(tokens):
+        for t in tokens:
+            if t == "E":
+                step(0, 3)
+            elif t == "L":
+                step(3, 6)
+            elif t[0] == "p":
+                step(int(t[1]), int(t[1]) + 1)
+            elif t[0] == "B":
+                n = int(t[1])
+                give(max(1, 16 * n), 16 * n + 16)
+            elif t == "edges":
+                finish_edges()
+            else:
+                finish_nodes()
+
+    act(PLAN[0])
 
     load_ecot.wait()
     carry[...] = jnp.zeros_like(carry)
@@ -407,7 +470,7 @@
     gloc[...] = dagg[1].astype(F32)
 
     def backward(i, _):
-        r = rows(i * CH, CH)
+        r = rows(i * 512, 512)
         scaled = xhat[r]
         mcot = ecot[r] + two(orecv[r], (agg[...].astype(BF16), gloc[...].astype(BF16)))
         carry[0:1] += jnp.sum(mcot * scaled, axis=0, keepdims=True)
@@ -429,8 +492,8 @@
         dpl[r] = dpre[1]
         return 0
 
-    lax.fori_loop(0, EDGES // CH, backward, 0)
-    next(rotations[0])
+    lax.fori_loop(0, 2, backward, 0)
+    act(PLAN[1])
     load_edge = load(edge_h, pre, 12)
 
     def scatter(first):
@@ -439,12 +502,13 @@
         return two(oslot[0:256, 0:EDGES], (dph[...], dpl[...]))
 
     def plane(n, _):
-        dz_ = (n + 1) % 4
-        at = (z + dz_) % 4 * 256
+        at = (z + n) % 4 * 256
         sbuf[rows(at, 256)] = scatter(NODES + at)
-
-        def give(i, _):
-            w, nn = peer(dz_ * 32 + i * 13 % 32)
+        return 0
+
+    def give(first, last):
+        def one(i, _):
+            w, nn = peer(i * 37 % 128)
             pltpu.make_async_remote_copy(
                 src_ref=sbuf.at[rows((w * 8 + nn) * 8, 8)],
                 dst_ref=abuf.at[mine8],
@@ -455,11 +519,10 @@
             ).start()
             return 0
 
-        lax.fori_loop(jnp.where(dz_ == 0, 1, 0), 32, give, 0)
-        return 0
+        lax.fori_loop(first, last, one, 0)
 
     lax.fori_loop(0, 4, plane, 0)
-    next(rotations[0])
+    act(PLAN[2])
     abuf[mine8] = sbuf[mine8]
     gloc[...] = scatter(0)
     rsum[...] = sum(
@@ -480,11 +543,12 @@
         lax.fori_loop(0, 4, part, 0)
 
     tall(UNITS["w2"], (hh, hl), (tabh, tabl), EDGES)
+    act(PLAN[3])
     rcut = split(rsum[...])
     put(UNITS["w1c"], three(dot_tn, node_pair(), rcut))
-    next(rotations[0])
-    next(rotations[1])
+    act(PLAN[4])
     tall(UNITS["w1b"], (sh, sl), (dph, dpl), EDGES)
+    act(PLAN[5])
     load_edge.wait()
 
     def cut_edges(i, _):
@@ -503,55 +567,30 @@
     buf[small : small + 1024] = jnp.zeros((1024, 128), F32)
     for q in range(4):
         buf[small + 8 * q : small + 8 * q + 8] = vectors[:, q * 128 : q * 128 + 128]
-    next(rotations[2])
 
     def edge_out(i, _):
         r = rows(i * CH, CH)
         ecot[r] += three(dot_nt, (dph[r], dpl[r]), weight("w1a"))
         return 0
 
-    lax.fori_loop(0, EDGES // CH, edge_out, 0)
-    store_edges = load(ecot, edge_grad_h, 13)
-    ncot[...] += three(dot_nt, rcut, weight("w1c"))
-
-    live = list(rotations)
-
-    def step():
-        for t in list(live):
-            if next(t, 0) == 0:
-                live.remove(t)
-
-    for _ in range(BEFORE):
-        step()
-    wait(abuf.at[pl.ds(0, 1016)], recv2)
+    def finish_edges():
+        lax.fori_loop(0, EDGES // CH, edge_out, 0)
+        stores.append(load(ecot, edge_grad_h, 13))
+        ncot[...] += three(dot_nt, rcut, weight("w1c")) + three(dot_nt, dpre, weight("nw1a"))
 
     def collect(i, _):
         gloc[...] += two(osend_t[i], split(abuf[rows(i * 256, 256)]))
         return 0
 
-    lax.fori_loop(0, 4, collect, 0)
-    ncot[...] += three(dot_nt, split(gloc[...]), weight("w1b"))
-    store_grad = load(ncot, node_grad_h, 14)
-    while live:
-        step()
-    stores = [store_nodes, store_edges, store_grad]
-    k = 15
-    for name, ref, at in (
-        ("w1a", w1g_h, 0),
-        ("w1b", w1g_h, 512),
-        ("w1c", w1g_h, 1024),
-        ("w2", w2g_h, 0),
-        ("nw1a", nw1g_h, 0),
-        ("nw1b", nw1g_h, 512),
-        ("nw2", nw2g_h, 0),
-    ):
-        for q in range(4):
-            src = out.at[pl.ds((UNITS[name] + q) * 512, 512)]
-            stores.append(load(src, ref.at[pl.ds(at, 512), pl.ds(q * 128, 128)], k))
-            k += 1
-    for q in range(4):
-        stores.append(load(out.at[pl.ds(small + 8 * q, 8)], small_h.at[:, pl.ds(q * 128, 128)], k))
-        k += 1
+    def finish_nodes():
+        wait(abuf.at[pl.ds(0, 1016)], recv2)
+        lax.fori_loop(0, 4, collect, 0)
+        ncot[...] += three(dot_nt, split(gloc[...]), weight("w1b"))
+        stores.append(load(ncot, node_grad_h, 14))
+
+    act(PLAN[6])
+    while due:
+        step(0, 6)
     wait(sbuf.at[pl.ds(0, 1016)], send2)
     for d in started:
         d.wait_send()
@@ -559,7 +598,58 @@
         d.wait()
 
 
-BEFORE = 4
+PLAN = (
+    ("E",),
+    ("E",),
+    ("B0",),
+    ("E", "B1",),
+    ("p3",),
+    ("E", "B2", "p4",),
+    ("p5", "E", "B3", "edges", "E", "B4", "L", "E", "B5", "L", "E", "B6", "L", "E", "B7", "L", "E", "L", "nodes",),
+)
+
+
+def place(*refs):
+    source, target, sems = refs[:4], refs[4:15], refs[15:17]
+    flat, near = refs[17], refs[18:]
+    moves = []
+
+    def move(src, mid, dst):
+        n = len(moves)
+        moves.append(
+            (
+                pltpu.make_async_copy(src, mid, sems[0].at[n]),
+                pltpu.make_async_copy(mid, dst, sems[1].at[n]),
+            )
+        )
+        moves[-1][0].start()
+
+    first = UNITS["small"] * 512
+    for i, k in enumerate((4, 6, 8, 10)):
+        for q in range(4):
+            r = first + 8 * q + i
+            move(source[3].at[r], flat.at[r], target[k].at[pl.ds(q * 128, 128)])
+    for k in range(3):
+        move(source[k], near[k], target[k])
+    for name, k, at in (
+        ("w1a", 3, 0),
+        ("w1b", 3, 512),
+        ("w1c", 3, 1024),
+        ("w2", 5, 0),
+        ("nw1a", 7, 0),
+        ("nw1b", 7, 512),
+        ("nw2", 9, 0),
+    ):
+        for q in range(4):
+            r = pl.ds((UNITS[name] + q) * 512, 512)
+            move(
+                source[3].at[r], flat.at[r], target[k].at[pl.ds(at, 512), pl.ds(q * 128, 128)]
+            )
+    for inward, outward in moves:
+        inward.wait()
+        outward.start()
+    for inward, outward in moves:
+        outward.wait()
 
 
 def local(
@@ -579,7 +669,6 @@
     node_w2,
     node_gain,
 ):
-    vectors = jnp.stack([edge_b1, edge_gain, node_b1, node_gain])
     shape = lambda *s: jax.ShapeDtypeStruct(s, F32)
     v32 = lambda *s: pltpu.VMEM(s, F32)
     v16 = lambda *s: pltpu.VMEM(s, BF16)
@@ -591,15 +680,12 @@
             shape(NODES, W),
             shape(NODES, W),
             shape(EDGES, W),
-            shape(1536, W),
-            shape(512, W),
-            shape(1024, W),
-            shape(512, W),
-            shape(8, W),
+            shape(FLAT, 128),
         ),
-        in_specs=[near] * 4 + [anywhere] * 8,
-        out_specs=[anywhere] * 8,
+        in_specs=[near] * 3 + [anywhere] * 12,
+        out_specs=[anywhere] * 4,
         scratch_shapes=[
+            v32(4, W),
             v32(NODES, W),
             v16(NODES, W),
             v16(NODES, W),
@@ -632,14 +718,14 @@
             v32(NODES, W),
             v32(FLAT, 128),
             v32(FLAT, 128),
-            v32(3, 2520, 128),
-            pltpu.SemaphoreType.DMA((48,)),
+            v32(7560, 128),
+            pltpu.SemaphoreType.DMA((32,)),
             pltpu.SemaphoreType.DMA,
             pltpu.SemaphoreType.DMA,
             pltpu.SemaphoreType.DMA,
             pltpu.SemaphoreType.DMA,
-            pltpu.SemaphoreType.DMA((3, SEMS)),
-            pltpu.SemaphoreType.DMA((3, SEMS)),
+            pltpu.SemaphoreType.DMA((6, SEMS)),
+            pltpu.SemaphoreType.DMA((6, SEMS)),
         ],
         compiler_params=pltpu.CompilerParams(
             collective_id=1, has_side_effects=True, vmem_limit_bytes=63 << 20
@@ -648,7 +734,10 @@
         edge_slot.reshape(8, 128),
         edge_receiver.reshape(8, 128),
         send_rows.reshape(8, 128),
-        vectors,
+        edge_b1,
+        edge_gain,
+        node_b1,
+        node_gain,
         node_latent,
         edge_latent,
         node_cotangent,
@@ -658,20 +747,33 @@
         node_w1,
         node_w2,
     )
-    new_nodes, node_grad, edge_grad, w1g, w2g, nw1g, nw2g, small = result
-    return (
-        new_nodes,
-        node_grad,
-        edge_grad,
-        w1g,
-        small[0],
-        w2g,
-        small[1],
-        nw1g,
-        small[2],
-        nw2g,
-        small[3],
-    )
+    return pl.pallas_call(
+        place,
+        out_shape=(
+            shape(NODES, W),
+            shape(NODES, W),
+            shape(EDGES, W),
+            shape(1536, W),
+            shape(512),
+            shape(512, W),
+            shape(512),
+            shape(1024, W),
+            shape(512),
+            shape(512, W),
+            shape(512),
+        ),
+        in_specs=[anywhere] * 4,
+        out_specs=(anywhere,) * 11,
+        scratch_shapes=[
+            pltpu.SemaphoreType.DMA((47,)),
+            pltpu.SemaphoreType.DMA((47,)),
+            v32(FLAT, 128),
+            v32(NODES, W),
+            v32(NODES, W),
+            v32(EDGES, W),
+        ],
+        compiler_params=pltpu.CompilerParams(vmem_limit_bytes=60 << 20),
+    )(*result)
 
 
 def solution(mesh):

time: 192 us -> 144 us (0.75)
  Pallas kernels: 173 us -> 141 us
  local copies, waits for them, and re-layouts: 16.2 us -> 1.47 us
    pallas_call x1, Pallas kernels: 173 us -> 133 us  [local(): pl.pallas_call(kernel, out_shape=(shape(NODES, W), shape(NODES, W), shape...]
    unnamed x18 -> x1, local copies, waits for them, and re-layouts: 14 us -> 0.79 us
    pallas_call x0 -> x1, Pallas kernels: none -> 8.46 us  [local(): pl.pallas_call(place, out_shape=(shape(NODES, W), shape(NODES, W), shape(...]
where the time goes in v1:
time: 144 us
  Pallas kernels  141 us (98%)
  local copies, waits for them, and re-layouts  1.47 us (1%)
    pallas_call x1, Pallas kernels, local(): pl.pallas_call(kernel, out_shape=(shape(NODES, W), shape(NODES, W), shape...  133 us
    pallas_call x1, Pallas kernels, local(): pl.pallas_call(place, out_shape=(shape(NODES, W), shape(NODES, W), shape(...  8.46 us

profile of v1, /device:TPU:1, one launch (start us, length us, event | category | flops | bytes accessed | tf_op | source)
XLA Modules:
  0.0 143.6 jit_solution(12578561814973943364)
XLA Ops:
  0.6 0.8 copy.27
  1.4 0.7 reshape.33.list_ref
  2.1 132.9 %shard_map.230 = (f32[256,512]{1,0:T(8,128)}, f32[256,512]{1,0:T(8,128)}, f32[1024,512]{1,0:T(8,128)}, f32[15360,128]{1,0:T(8,128)}) custom-call(s32[8,128]{1,0:T(8,128)} %bitcast.2, s32[8,128]{1,0:T(8,128)} %bitcast.3, s32[8,128]{1,0:T(8,128)} %reshape.33.list_ref, f32[512]{0:T(512)} %eb1_h.1, f32[512]{0:T(512)} %eg_h.1, f32[512]{0:T(512)} %nb1_h.1, ...), custom_call_target="tpu_custom_call" | custom-call | tf_op jit(solution)/shard_map/pallas_call | solution.py:677
  135.0 8.5 %shard_map.231 = (f32[256,512]{1,0:T(8,128)}, f32[256,512]{1,0:T(8,128)}, f32[1024,512]{1,0:T(8,128)}, f32[1536,512]{1,0:T(8,128)}, f32[512]{0:T(512)}, /*index=...) custom-call(f32[256,512]{1,0:T(8,128)} %get-tuple-element.15.refs_0_, ...), custom_call_target="tpu_custom_call" | custom-call | tf_op jit(solution)/shard_map/pallas_call | solution.py:750

commit v2 on v1

--- a/solution.py
+++ b/solution.py
@@ -599,13 +599,13 @@
 
 
 PLAN = (
-    ("E",),
-    ("E",),
-    ("B0",),
-    ("E", "B1",),
-    ("p3",),
-    ("E", "B2", "p4",),
-    ("p5", "E", "B3", "edges", "E", "B4", "L", "E", "B5", "L", "E", "B6", "L", "E", "B7", "L", "E", "L", "nodes",),
+    ("E", ),
+    ("E", ),
+    ("B0", ),
+    ("E", "B1", ),
+    ("p3", ),
+    ("E", "p4", ),
+    ("p5", "E", "B2", "edges", "E", "L", "E", "B3", "L", "B4", "E", "L", "B5", "E", "L", "B6", "E", "L", "B7", "E", "L", "L", "L", "nodes", ),
 )
 
 

time: 144 us -> 142 us (0.986)
  Pallas kernels: 141 us -> 139 us
    pallas_call x1, Pallas kernels: 133 us -> 131 us  [local(): pl.pallas_call(kernel, out_shape=(shape(NODES, W), shape(NODES, W), shape...]
where the time goes in v2:
time: 142 us
  Pallas kernels  139 us (98%)
  local copies, waits for them, and re-layouts  1.47 us (1%)
    pallas_call x1, Pallas kernels, local(): pl.pallas_call(kernel, out_shape=(shape(NODES, W), shape(NODES, W), shape...  131 us
    pallas_call x1, Pallas kernels, local(): pl.pallas_call(place, out_shape=(shape(NODES, W), shape(NODES, W), shape(...  8.46 us

profile of v2, /device:TPU:1, one launch (start us, length us, event | category | flops | bytes accessed | tf_op | source)
XLA Modules:
  0.0 141.7 jit_solution(2477880997479811106)
XLA Ops:
  0.6 0.8 copy.27
  1.4 0.7 reshape.33.list_ref
  2.1 130.9 %shard_map.230 = (f32[256,512]{1,0:T(8,128)}, f32[256,512]{1,0:T(8,128)}, f32[1024,512]{1,0:T(8,128)}, f32[15360,128]{1,0:T(8,128)}) custom-call(s32[8,128]{1,0:T(8,128)} %bitcast.2, s32[8,128]{1,0:T(8,128)} %bitcast.3, s32[8,128]{1,0:T(8,128)} %reshape.33.list_ref, f32[512]{0:T(512)} %eb1_h.1, f32[512]{0:T(512)} %eg_h.1, f32[512]{0:T(512)} %nb1_h.1, ...), custom_call_target="tpu_custom_call" | custom-call | tf_op jit(solution)/shard_map/pallas_call | solution.py:677
  133.0 8.5 %shard_map.231 = (f32[256,512]{1,0:T(8,128)}, f32[256,512]{1,0:T(8,128)}, f32[1024,512]{1,0:T(8,128)}, f32[1536,512]{1,0:T(8,128)}, f32[512]{0:T(512)}, /*index=...) custom-call(f32[256,512]{1,0:T(8,128)} %get-tuple-element.15.refs_0_, ...), custom_call_target="tpu_custom_call" | custom-call | tf_op jit(solution)/shard_map/pallas_call | solution.py:750

commit v3 on v2

--- a/solution.py
+++ b/solution.py
@@ -66,11 +66,15 @@
 
 
 def three(op, a, b):
-    return op(a[0], b[0]) + op(a[1], b[0]) + op(a[0], b[1])
+    ka = 0 if op is dot_tn else 1
+    kb = 1 if op is dot_nt else 0
+    return op(jnp.concatenate([a[0], a[1], a[0]], axis=ka), jnp.concatenate([b[0], b[0], b[1]], axis=kb))
 
 
 def two(one_hot, pair):
-    return dot(one_hot, pair[0]) + dot(one_hot, pair[1])
+    return dot(
+        jnp.concatenate([one_hot, one_hot], axis=1), jnp.concatenate([pair[0], pair[1]], axis=0)
+    )
 
 
 def reduce_part(part, buf, out, halves_in, send, recv, started):
@@ -532,10 +536,8 @@
     def tall(unit, a, b, n):
         def part(i, _):
             lanes = pl.ds(pl.multiple_of(i * 128, 128), 128)
-            value = (
-                dot_tn(a[0][:, lanes], b[0][pl.ds(0, n)])
-                + dot_tn(a[1][:, lanes], b[0][pl.ds(0, n)])
-                + dot_tn(a[0][:, lanes], b[1][pl.ds(0, n)])
+            value = three(
+                dot_tn, (a[0][:, lanes], a[1][:, lanes]), (b[0][pl.ds(0, n)], b[1][pl.ds(0, n)])
             )
             put(unit, value, i * 128)
             return 0
@@ -605,7 +607,7 @@
     ("E", "B1", ),
     ("p3", ),
     ("E", "p4", ),
-    ("p5", "E", "B2", "edges", "E", "L", "E", "B3", "L", "B4", "E", "L", "B5", "E", "L", "B6", "E", "L", "B7", "E", "L", "L", "L", "nodes", ),
+    ("p5", "E", "B2", "edges", "L", "E", "L", "E", "B3", "L", "E", "B4", "L", "E", "B5", "L", "E", "B6", "L", "E", "B7", "L", "L", "nodes", ),
 )
 
 

time: 142 us -> 142 us (level)
  no operation moved by 1% of the time
where the time goes in v3:
time: 142 us; the launch traced here: 141 us
  Pallas kernels  139 us (98%)
  local copies, waits for them, and re-layouts  1.47 us (1%)
    pallas_call x1, Pallas kernels, local(): pl.pallas_call(kernel, out_shape=(shape(NODES, W), shape(NODES, W), shape...  131 us
    pallas_call x1, Pallas kernels, local(): pl.pallas_call(place, out_shape=(shape(NODES, W), shape(NODES, W), shape(...  8.46 us

profile of v3, /device:TPU:1, one launch (start us, length us, event | category | flops | bytes accessed | tf_op | source)
XLA Modules:
  0.0 141.3 jit_solution(1372649691190834274)
XLA Ops:
  0.6 0.8 copy.27
  1.4 0.7 reshape.33.list_ref
  2.1 130.6 %shard_map.230 = (f32[256,512]{1,0:T(8,128)}, f32[256,512]{1,0:T(8,128)}, f32[1024,512]{1,0:T(8,128)}, f32[15360,128]{1,0:T(8,128)}) custom-call(s32[8,128]{1,0:T(8,128)} %bitcast.2, s32[8,128]{1,0:T(8,128)} %bitcast.3, s32[8,128]{1,0:T(8,128)} %reshape.33.list_ref, f32[512]{0:T(512)} %eb1_h.1, f32[512]{0:T(512)} %eg_h.1, f32[512]{0:T(512)} %nb1_h.1, ...), custom_call_target="tpu_custom_call" | custom-call | tf_op jit(solution)/shard_map/pallas_call | solution.py:679
  132.7 8.5 %shard_map.231 = (f32[256,512]{1,0:T(8,128)}, f32[256,512]{1,0:T(8,128)}, f32[1024,512]{1,0:T(8,128)}, f32[1536,512]{1,0:T(8,128)}, f32[512]{0:T(512)}, /*index=...) custom-call(f32[256,512]{1,0:T(8,128)} %get-tuple-element.15.refs_0_, ...), custom_call_target="tpu_custom_call" | custom-call | tf_op jit(solution)/shard_map/pallas_call | solution.py:752
